TPU v7x, 768 devices: a whole 4x8x12 slice. The times are simulated.
768 devices in a mesh: row: 64 (over y, x, core), col: 12 (over z).
Axes of the slice: x: 4, y: 8, z: 12, core: 2. Of those that a mesh axis runs over, the one named last changes fastest.
Arguments:
- slab_amps: bfloat16 [64, 49152], P('row', 'col'), may hold values from -6 to 6
- lad_ints: bfloat16 [294912, 4096], P(('row', 'col')), may hold values from -0.0546875 to 0.0546875
- lad_pairs: int32 [294912], P(('row', 'col')), may hold values from 0 to 1535, as said below
- cycle_amps: bfloat16 [49152, 4096], P(('row', 'col')), may hold values from -6 to 6
- cycle_dest: int32 [49152, 1], P(('row', 'col')), may hold values from 0 to 63; in each aligned block of 64 rows (0 to 63, 64 to 127, ...) at most 2 rows name the same one
- cycle_block: int32 [49152], P(('row', 'col')), may hold values from 0 to 3
- cycle_kblk: int32 [49152], P(('row', 'col')), may hold values from 0 to 15
- cycle_ints: bfloat16 [12288, 1536], P('col'), may hold values from -0.0546875 to 0.0546875
Outputs:
- ladder_residual: float32 [64, 98304], P(None, ('row', 'col'))
- cycle_residual: float32 [16384, 1536], P('row', 'col')
Inputs may be any that keep to these rules, and one draw needn't show every extreme that they name: `lad_pairs`: within each device's block of 384 entries the values are distinct; they encode p * 24 + q. `cycle_dest`: within the rows of one device (aligned blocks of 64) no owner is named by more than 2 rows.
All inputs are finite; a program needn't handle non-finite values.
Results may differ from a plain program's by a relative error of at most 0.0024.
Values may be sent and summed in bfloat16 or wider, within the bound.
A program may use at most 192 MiB of HBM per device.

v0:
```python
import jax
import jax.numpy as jnp
from jax import lax
from jax.sharding import PartitionSpec as P

TILE = 64
P_DEV = 64
Q_DEV = 24
W_DEV = 384
S_DEV = 64
M_DEV = 4
NK_DEV = 16


def local(
    slab_amps, lad_ints, lad_pairs, cycle_amps, cycle_dest, cycle_block, cycle_kblk, cycle_ints
):
    weight_tiles = lad_ints.reshape(W_DEV, TILE, TILE)
    p_block = lad_pairs // Q_DEV
    q_block = lad_pairs % Q_DEV
    picker = (q_block[:, None] == jnp.arange(Q_DEV, dtype=jnp.int32)[None, :]).astype(jnp.float32)
    rows_in = lax.all_gather(slab_amps, "row", axis=0, tiled=True)
    row_count = rows_in.shape[0]
    tile_rows = rows_in.reshape(row_count, P_DEV, TILE)[:, p_block, :]
    products = jnp.einsum(
        "ksx,sxy->ksy", tile_rows, weight_tiles, preferred_element_type=jnp.float32
    )
    summed = jnp.einsum("sq,ksy->kqy", picker, products, precision=lax.Precision.HIGHEST)
    ladder_part = summed.reshape(row_count, Q_DEV * TILE)
    row_devices = lax.axis_size("row")
    capacity = max(2, 2 * S_DEV // row_devices)
    owners = cycle_dest[:, 0]
    owner_hits = (owners[:, None] == jnp.arange(row_devices, dtype=jnp.int32)[None, :]).astype(
        jnp.int32
    )
    before = jnp.cumsum(owner_hits, axis=0) - owner_hits
    position = jnp.sum(before * owner_hits, axis=1)
    send_slot = owners * capacity + position
    outgoing = (
        jnp.zeros((row_devices * capacity, TILE * TILE), jnp.bfloat16).at[send_slot].set(cycle_amps)
    )
    cell_codes = (
        jnp.full((row_devices * capacity,), -1, jnp.int32)
        .at[send_slot]
        .set(cycle_block * NK_DEV + cycle_kblk)
    )
    arrived, arrived_codes = (
        lax.all_to_all(
            outgoing.reshape(row_devices, capacity, TILE * TILE),
            "row",
            split_axis=0,
            concat_axis=0,
            tiled=True,
        ),
        lax.all_to_all(
            cell_codes.reshape(row_devices, capacity),
            "row",
            split_axis=0,
            concat_axis=0,
            tiled=True,
        ),
    )
    arrived = arrived.reshape(row_devices * capacity, TILE * TILE)
    arrived_codes = arrived_codes.reshape(row_devices * capacity)
    placer = (
        jnp.arange(M_DEV * NK_DEV, dtype=jnp.int32)[:, None] == arrived_codes[None, :]
    ).astype(jnp.bfloat16)
    cell_sums = jnp.dot(placer, arrived, preferred_element_type=jnp.float32).astype(jnp.bfloat16)
    cycle_slab = cell_sums.reshape(M_DEV, NK_DEV, TILE, TILE).transpose(0, 2, 1, 3)
    cycle_slab = cycle_slab.reshape(M_DEV * TILE, NK_DEV * TILE)
    cycle_part = jnp.dot(cycle_slab, cycle_ints, preferred_element_type=jnp.float32)
    ladder_out = lax.psum_scatter(ladder_part, "col", scatter_dimension=1, tiled=True)
    cycle_out = lax.psum_scatter(cycle_part, "col", scatter_dimension=1, tiled=True)
    return (ladder_out, cycle_out)


def solution(mesh):
    in_specs = (
        P("row", "col"),
        P(("row", "col"), None),
        P(("row", "col")),
        P(("row", "col"), None),
        P(("row", "col"), None),
        P(("row", "col")),
        P(("row", "col")),
        P("col", None),
    )
    out_specs = (P(None, ("row", "col")), P("row", "col"))
    return jax.shard_map(local, mesh=mesh, in_specs=in_specs, out_specs=out_specs, check_vma=False)
```

profile of v0, /device:TPU:10, one launch (start us, length us, event | category | flops | bytes accessed | tf_op | source)
XLA Modules:
  0.0 294.4 jit_solution(8101596613204667535)
XLA Ops:
  7.2 0.0 copy-start
  7.2 0.9 fusion.14
  8.1 0.1 reduce_window_sum.11
  8.2 0.8 select_reduce_fusion
  9.0 0.7 fusion.18
  9.7 0.7 multiply_add_fusion
  10.3 0.8 scatter_custom_fusion
  11.1 0.8 all_to_all.9
  11.9 13.5 %all-to-all-start = ((s32[64,1,2]{2,1,0:T(1,128)}), s32[64,1,2]{2,1,0:T(1,128)S(1)}, u32[]{:S(2)}, u32[]{:S(2)}) async-start(s32[64,1,2]{2,1,0:T(1,128)} %bitcast.9), calls=%async_computation.1 | async-start | bytes 65536 | tf_op jit(solution)/shard_map/all_to_all | solution.py:55
  25.4 4.7 %copy.14 = bf16[384,4096]{0,1:T(8,128)(2,1)} copy(bf16[384,4096]{1,0:T(8,128)(2,1)} %param.9) | data formatting | bytes 6291456 | tf_op args[1]
  30.1 0.0 copy-start.1
  30.1 10.3 %copy.15 = bf16[384,64,64]{2,1,0:T(8,128)(2,1)} copy(bf16[384,64,64]{0,2,1:T(8,128)(2,1)} %bitcast.31) | data formatting | bytes 6291456 | tf_op jit(solution)/shard_map/reshape | solution.py:18
  40.4 0.0 copy-start.2
  40.4 2.9 scatter_custom_fusion.1
  43.4 2.5 reshape.36
  45.9 0.0 all-to-all-done
  45.9 10.5 %all-to-all-start.1 = ((bf16[64,2,4096]{2,1,0:T(2,128)(2,1)}), bf16[64,2,4096]{2,1,0:T(2,128)(2,1)}, u32[]{:S(2)}, u32[]{:S(2)}) async-start(bf16[64,2,4096]{2,1,0:T(2,128)(2,1)} %reshape.36), calls=%async_computation.2 | async-start | bytes 2097152 | tf_op jit(solution)/shard_map/all_to_all | solution.py:48
  56.4 0.0 reduce-scatter.3.cloned.1.call-start
  56.5 0.0 copy-done.1
  56.5 72.5 %all-gather = bf16[64,1,4096]{2,1,0:T(2,128)(2,1)} all-gather(bf16[1,1,4096]{2,1,0:T(2,128)(2,1)S(1)} %bitcast.33), channel_id=1, replica_groups=mesh['row'=64,'col'=12] {'row'}, dimensions={0}, use_global_device_ids=true | all-gather | bytes 532480 | tf_op jit(solution)/shard_map/all_gather | solution.py:22
  129.0 5.1 %reduce = bf16[64,4096]{1,0:T(8,128)(2,1)} reduce(bf16[64,1,4096]{2,1,0:T(2,128)(2,1)} %all-gather, bf16[]{:T(256)} %constant.46), dimensions={1}, to_apply=%all-gather.reduce_sub_computation | reduce | bytes 1048578 | tf_op jit(solution)/shard_map/all_gather | solution.py:22
  134.1 2.8 reshape.33
  136.9 2.9 copy.13
  139.8 0.0 copy-done.2
  139.8 5.3 %gather_fusion = bf16[384,64,64]{2,1,0:T(8,128)(2,1)} fusion(bf16[64,64,64]{2,0,1:T(8,128)(2,1)} %copy.13, s32[1024]{0:T(1024)S(1)} %pad_clamp_fusion), kind=kCustom, calls=%fused_computation | custom fusion | bytes 6292992 | tf_op jit(solution)/shard_map/gather | solution.py:24
  145.0 6.4 %fusion.4 = f32[64,384,64]{2,0,1:T(8,128)S(1)} fusion(bf16[384,64,64]{2,1,0:T(8,128)(2,1)} %copy.15, bf16[384,64,64]{2,1,0:T(8,128)(2,1)} %gather_fusion), kind=kOutput, calls=%fused_computation.8 | convolution fusion | flops 201326592 | bytes 12582912 | tf_op jit(solution)/shard_map/ksx,sxy->ksy/dot_general | solution.py:25
  151.4 12.3 %fusion.7 = f32[64,24,64]{2,1,0:T(8,128)} fusion(f32[64,384,64]{2,0,1:T(8,128)S(1)} %fusion.4, s32[384]{0:T(512)S(1)} %get-tuple-element.2), kind=kOutput, calls=%fused_computation.9 | convolution fusion | flops 452994048 | bytes 6686208 | tf_op jit(solution)/shard_map/sq,ksy->kqy/dot_general | solution.py:28
  163.8 2.1 reshape.35
  165.9 0.0 reduce-scatter.3.cloned.1.call-update
  165.9 0.0 reduce-scatter.5.cloned.1.call-start
  165.9 0.5 broadcast.30
  166.5 0.7 reduce.4
  167.2 0.1 eq.53
  167.3 0.0 all-to-all-done.1
  167.3 2.3 reshape.37
  169.6 2.3 convolution_convert_fusion
  171.9 2.8 reshape.38
  174.7 2.9 copy.24
  177.6 2.6 reshape.39
  180.2 0.0 copy-done
  180.2 3.2 %fusion.21 = f32[256,1536]{1,0:T(8,128)} fusion(bf16[256,1024]{1,0:T(8,128)(2,1)} %reshape.39, bf16[1024,1536]{1,0:T(8,128)(2,1)S(1)} %copy-done), kind=kOutput, calls=%fused_computation.34 | convolution fusion | flops 805306368 | bytes 5242880 | tf_op jit(solution)/shard_map/dot_general | solution.py:71
  183.4 0.0 reduce-scatter.5.cloned.1.call-update
  183.4 42.0 %reduce-scatter.3.cloned.1.call-done = f32[64,128]{1,0:T(8,128)} async-done(((f32[64,1536]{1,0:T(8,128)}), f32[64,128]{1,0:T(8,128)}) %reduce-scatter.3.cloned.1.call-update) | async-done | bytes 32784 | tf_op jit(solution)/shard_map/reduce_scatter | solution.py:72
  225.5 62.1 %reduce-scatter.5.cloned.1.call-done = f32[256,128]{1,0:T(8,128)} async-done(((f32[256,1536]{1,0:T(8,128)}), f32[256,128]{1,0:T(8,128)}) %reduce-scatter.5.cloned.1.call-update) | async-done | bytes 131088 | tf_op jit(solution)/shard_map/reduce_scatter | solution.py:73
  (2 shorter events, 0.0 us)
Async XLA Ops:
  7.2 173.1 %copy-start = (bf16[1024,1536]{1,0:T(8,128)(2,1)S(1)}, bf16[1024,1536]{1,0:T(8,128)(2,1)}, u32[]{:S(2)}) copy-start(bf16[1024,1536]{1,0:T(8,128)(2,1)} %param.15) | copy-start | bytes 9437188
  11.9 34.0 %all-to-all-start = ((s32[64,1,2]{2,1,0:T(1,128)}), s32[64,1,2]{2,1,0:T(1,128)S(1)}, u32[]{:S(2)}, u32[]{:S(2)}) async-start(s32[64,1,2]{2,1,0:T(1,128)} %bitcast.9), calls=%async_computation.1 | async-start | bytes 65536 | tf_op jit(solution)/shard_map/all_to_all | solution.py:55
  30.1 26.3 %copy-start.1 = (bf16[1,4096]{1,0:T(2,128)(2,1)S(1)}, bf16[1,4096]{1,0:T(2,128)(2,1)}, u32[]{:S(2)}) copy-start(bf16[1,4096]{1,0:T(2,128)(2,1)} %param.8) | copy-start | bytes 24580
  40.4 99.3 %copy-start.2 = (s32[384]{0:T(512)S(1)}, s32[384]{0:T(512)}, u32[]{:S(2)}) copy-start(s32[384]{0:T(512)} %param.10) | copy-start | bytes 4612
  45.9 121.4 %all-to-all-start.1 = ((bf16[64,2,4096]{2,1,0:T(2,128)(2,1)}), bf16[64,2,4096]{2,1,0:T(2,128)(2,1)}, u32[]{:S(2)}, u32[]{:S(2)}) async-start(bf16[64,2,4096]{2,1,0:T(2,128)(2,1)} %reshape.36), calls=%async_computation.2 | async-start | bytes 2097152 | tf_op jit(solution)/shard_map/all_to_all | solution.py:48
  56.4 169.0 %reduce-scatter.3.cloned.1.call-start = ((), (), s32[]{:S(2)}) async-start(), calls=%async_computation.4 | async-start | bytes 425984 | tf_op jit(solution)/shard_map/reduce_scatter | solution.py:72
  165.9 121.6 %reduce-scatter.5.cloned.1.call-start = ((), (), s32[]{:S(2)}) async-start(), calls=%async_computation.5 | async-start | bytes 1703936 | tf_op jit(solution)/shard_map/reduce_scatter | solution.py:73
Sparse Core Ops, SparseCore 0:
  166.0 59.3 reduce-scatter.2
  229.5 58.0 reduce-scatter.4
where the time goes:
time: 295 us; the launch traced here: 294 us
  waiting for transfers between devices  104 us (35%)
  blocking collectives  72.5 us (25%)
  local copies, waits for them, and re-layouts  46.2 us (16%)
  matrix products  24.2 us (8%)
  starting transfers between devices  24.1 us (8%)
  between operations  14.1 us (5%)
  other arithmetic  8.97 us (3%)
    all_gather x1, blocking collectives, local(): rows_in = lax.all_gather(slab_amps, 'row', axis=0, tiled=True)  72.5 us
    reduce_scatter x1, waiting for transfers between devices, local(): lax.psum_scatter(cycle_part, 'col', scatter_dimension=1, tiled=True)  62.1 us
    reduce_scatter x1, waiting for transfers between devices, local(): lax.psum_scatter(ladder_part, 'col', scatter_dimension=1, tiled=True)  42 us
    all_to_all x1, starting transfers between devices, local(): lax.all_to_all(cell_codes.reshape(row_devices, capacity), 'row', split_ax...  13.5 us
    dot_general x1, matrix products, local(): jnp.einsum('sq,ksy->kqy', picker, products, precision=lax.Precision.HIGHEST)  12.3 us
    all_to_all x1, starting transfers between devices, local(): lax.all_to_all(outgoing.reshape(row_devices, capacity, TILE * TILE), 'row...  10.5 us
    reshape x1, local copies, waits for them, and re-layouts, local(): weight_tiles = lad_ints.reshape(W_DEV, TILE, TILE)  10.3 us
    dot_general x1, matrix products, local(): jnp.einsum('ksx,sxy->ksy', tile_rows, weight_tiles, preferred_element_typ...  6.39 us
  transfers between devices with their start and end apart: 4, of which 2 were waited for; matrix products, arithmetic and copies ran while one was open for 25% of the time, Pallas kernels for 0%

commit v1 on v0

v1 whole, which is shorter than its diff:
```python
import jax
import jax.numpy as jnp
from jax import lax
from jax.experimental import pallas as pl
from jax.experimental.pallas import tpu as pltpu
from jax.sharding import PartitionSpec as P

MESH = pl.DeviceIdType.MESH
F32 = jnp.float32
BF16 = jnp.bfloat16
I32 = jnp.int32

NR = 64
NC = 12
NY, NX = 8, 4
TILES = 64
ENTRIES = 384
Q_DEV = 24
MSG = 48
SUB = 64
NSUB = 4
STEPS = 6


def dot(a, b):
    return jnp.dot(a, b, preferred_element_type=F32)


def iota(shape, dim):
    return lax.broadcasted_iota(I32, shape, dim)


def kernel(
    amps_ref, pairs_ref, dest_ref, block_ref, kblk_ref, w_hbm, cyc_hbm, b_hbm,
    lad_out, cyc_out,
    w_ref, cyc_ref, b_ref, stage, outgoing, arrived, gather, gstage, lad_lhs, placer, dense,
    lad_part, lad_slots, cells, cyc_lhs, part, slot_up, slot_dn, turn,
    local_sem, g1_send, g1_recv, g2_send, g2_recv, a_send, a_recv, l_send, l_recv,
    r_send, r_recv_up, r_recv_dn,
):
    me = lax.axis_index("row")
    col = lax.axis_index("col")
    my_y = me // 8
    my_x = lax.rem(me // 2, 4)
    my_core = lax.rem(me, 2)
    my_slot = my_y * 2 + my_core

    local = [
        pltpu.make_async_copy(cyc_hbm, cyc_ref, local_sem.at[0]),
        pltpu.make_async_copy(w_hbm, w_ref, local_sem.at[1]),
        pltpu.make_async_copy(b_hbm, b_ref, local_sem.at[2]),
    ]
    for copy in local:
        copy.start()

    barrier = pltpu.get_barrier_semaphore()

    def greet_row(k, carry):
        pl.semaphore_signal(
            barrier, inc=1, device_id={"row": lax.rem(me + k, NR)}, device_id_type=MESH
        )
        return carry

    def greet_col(k, carry):
        pl.semaphore_signal(
            barrier, inc=1, device_id={"col": lax.rem(col + k, NC)}, device_id_type=MESH
        )
        return carry

    lax.fori_loop(1, NR, greet_row, 0)
    lax.fori_loop(1, NC, greet_col, 0)

    flipped = amps_ref[...].astype(F32).T
    turn[:, 0:32] = flipped[0:64, :]
    turn[:, 32:64] = flipped[64:128, :]
    quarter = [[turn[pl.ds(2 * a1 + par, 16, stride=4), :] for a1 in (0, 1)] for par in (0, 1)]
    message = jnp.concatenate([jnp.concatenate(quarter[par], axis=1) for par in (0, 1)], axis=0)

    dest_col = dest_ref[...]
    eye = iota((TILES, TILES), 0) == iota((TILES, TILES), 1)
    dest_row = jnp.sum(jnp.where(eye, dest_col, 0), axis=0, keepdims=True)
    same = dest_col == dest_row
    earlier_col = iota((TILES, TILES), 0) < iota((TILES, TILES), 1)
    earlier_row = iota((TILES, TILES), 1) < iota((TILES, TILES), 0)
    pos_row = jnp.sum(jnp.where(same & earlier_col, 1, 0), axis=0, keepdims=True)
    pos_col = jnp.sum(jnp.where(same & earlier_row, 1, 0), axis=1, keepdims=True)
    code_row = block_ref[...] * 16 + kblk_ref[...]
    code_col = jnp.sum(jnp.where(eye, code_row, 0), axis=1, keepdims=True)
    slot_row = dest_row * 2 + pos_row
    slot_col = dest_col * 2 + pos_col
    chosen = (iota((2 * NR, TILES), 0) == slot_row).astype(F32).astype(BF16)
    codes = jnp.sum(
        jnp.where(iota((TILES, 2 * NR), 1) == slot_col, code_col + 1, 0), axis=0, keepdims=True
    ) - 1
    gather[my_x, my_slot, 0:32, :] = message.astype(BF16)
    gather[my_x, my_slot, 32:48, :] = jnp.where(
        iota((16, 128), 0) == 0, codes, 0
    ).astype(F32).astype(BF16)

    pl.semaphore_wait(barrier, NR - 1 + NC - 1)

    def first_stage(k):
        there = lax.rem(my_slot + k, 16)
        row = (there // 2) * 8 + my_x * 2 + lax.rem(there, 2)
        return there, pltpu.make_async_remote_copy(
            gather.at[my_x, my_slot], gather.at[my_x, my_slot], g1_send.at[k], g1_recv.at[my_slot],
            device_id={"row": row}, device_id_type=MESH,
        )

    def first_send(k, carry):
        first_stage(k)[1].start()
        return carry

    lax.fori_loop(1, 16, first_send, 0)

    local[0].wait()

    def stage_tiles(g, carry):
        picked = dot(chosen, cyc_ref[:, pl.ds(pl.multiple_of(g * 256, 256), 256)])
        stage[pl.ds(2 * g, 128, stride=32), :] = picked[:, 0:128]
        stage[pl.ds(2 * g + 1, 128, stride=32), :] = picked[:, 128:256]
        return carry

    lax.fori_loop(0, 16, stage_tiles, 0)

    def tile_copy(d):
        return pltpu.make_async_remote_copy(
            outgoing.at[d], arrived.at[me], a_send.at[d], a_recv.at[me],
            device_id={"row": d}, device_id_type=MESH,
        )

    def tile_send(k, carry):
        d = lax.rem(me + k, NR)
        outgoing[d] = stage[pl.ds(pl.multiple_of(d * 64, 64), 64), :].astype(BF16)
        tile_copy(d).start()
        return carry

    lax.fori_loop(1, NR, tile_send, 0)
    arrived[me] = stage[pl.ds(pl.multiple_of(me * 64, 64), 64), :].astype(BF16)

    def first_wait(k, carry):
        there = lax.rem(my_slot + k, 16)
        pltpu.make_async_remote_copy(
            gather.at[my_x, there], gather.at[my_x, there], g1_send.at[0], g1_recv.at[there],
            device_id={"row": lax.rem(me + 1, NR)}, device_id_type=MESH,
        ).wait_recv()
        return carry

    lax.fori_loop(1, 16, first_wait, 0)

    def second_copy(k, x):
        there = lax.rem(my_x + k, NX)
        return pltpu.make_async_remote_copy(
            gather.at[x], gather.at[x], g2_send.at[k], g2_recv.at[x],
            device_id={"row": my_y * 8 + there * 2 + my_core}, device_id_type=MESH,
        )

    for k in range(1, NX):
        second_copy(k, my_x).start()

    pairs = pairs_ref[...]
    p_at = iota((64, ENTRIES), 0)
    p_code = (2 * lax.rem(p_at, 32) + p_at // 32) * Q_DEV

    def build(q, carry):
        placer[pl.ds(pl.multiple_of(q * 64, 64), 64), :] = (
            (p_code + q == pairs).astype(F32).astype(BF16)
        )
        return carry

    lax.fori_loop(0, Q_DEV, build, 0)
    local[1].wait()

    def place(g, carry):
        w_part = w_ref[:, pl.ds(pl.multiple_of(g * 256, 256), 256)]
        for quarter_at in range(4):
            placed = dot(placer[quarter_at * 384:(quarter_at + 1) * 384, :], w_part).astype(BF16)
            for j in range(6):
                q = quarter_at * 6 + j
                for i in (0, 1):
                    dense[
                        q // 2, pl.ds(pl.multiple_of((2 * g + i) * 64, 64), 64),
                        (q % 2) * 128:(q % 2 + 1) * 128,
                    ] = placed[j * 64:(j + 1) * 64, i * 128:(i + 1) * 128]
        return carry

    lax.fori_loop(0, 16, place, 0)

    for k in range(1, NX):
        x = lax.rem(my_x + k, NX)
        second_copy(k, x).wait_recv()

    def widen(i, carry):
        x, rest = i // 16, lax.rem(i, 16)
        row = (rest // 2) * 8 + x * 2 + lax.rem(rest, 2)
        gstage[pl.ds(pl.multiple_of(row * MSG, MSG), MSG), :] = gather[x, rest].astype(F32)
        return carry

    lax.fori_loop(0, NR, widen, 0)
    for par in (0, 1):
        for b in range(16):
            lad_lhs[par * 64:(par + 1) * 64, b * 128:(b + 1) * 128] = (
                gstage[pl.ds(par * 16 + b, NR, stride=MSG), :].astype(BF16)
            )

    low = iota((64, 128), 1) < 64

    def lad_copy(k):
        c = lax.rem(col + k, NC)
        return pltpu.make_async_remote_copy(
            lad_part.at[c], lad_slots.at[k], l_send.at[k], l_recv.at[k],
            device_id={"col": c}, device_id_type=MESH,
        )

    def ladder(k):
        c = lax.rem(col + k, NC)
        acc = dot(lad_lhs[...], dense[c])
        first = acc[0:64, 0:128] + pltpu.roll(acc[64:128, 0:128], 64, 1)
        second = pltpu.roll(acc[0:64, 128:256], 64, 1) + acc[64:128, 128:256]
        lad_part[c] = jnp.where(low, first, second)

    def ladder_send(k, carry):
        ladder(k)
        lad_copy(k).start()
        return carry

    lax.fori_loop(1, NC, ladder_send, 0)
    ladder(0)

    all_codes = gstage[pl.ds(32, NR, stride=MSG), :]
    mine = []
    for j in (0, 1):
        here = jnp.where(iota((NR, 128), 1) == 2 * me + j, all_codes, 0.0)
        mine.append(jnp.sum(here, axis=1, keepdims=True))
    slot_codes = jnp.concatenate(mine, axis=0)
    put = (slot_codes == iota((2 * NR, 128), 1).astype(F32)).astype(F32).T[0:64, :].astype(BF16)

    def tile_wait(k, carry):
        s = lax.rem(me + NR - k, NR)
        pltpu.make_async_remote_copy(
            outgoing.at[s], arrived.at[s], a_send.at[s], a_recv.at[s],
            device_id={"row": lax.rem(me + k, NR)}, device_id_type=MESH,
        ).wait_recv()
        stage[pl.ds(pl.multiple_of(s * 64, 64), 64), :] = arrived[s].astype(F32)
        return carry

    stage[pl.ds(pl.multiple_of(me * 64, 64), 64), :] = arrived[me].astype(F32)
    lax.fori_loop(1, NR, tile_wait, 0)

    def cell(g, carry):
        wide = []
        for i in (0, 1):
            a = 2 * g + i
            wide.append(jnp.concatenate(
                [stage[pl.ds(a + 32 * j, NR, stride=64), :] for j in (0, 1)], axis=0
            ).astype(BF16))
        summed = dot(put, jnp.concatenate(wide, axis=1))
        cells[pl.ds(2 * g, 64, stride=32), :] = summed[:, 0:128]
        cells[pl.ds(2 * g + 1, 64, stride=32), :] = summed[:, 128:256]
        return carry

    lax.fori_loop(0, 16, cell, 0)

    low32 = iota((32, 128), 1) < 64

    def pair(i, carry):
        m, nn = i // 8, lax.rem(i, 8)
        at = pl.multiple_of((m * 16 + 2 * nn) * 32, 32)
        even = cells[pl.ds(at, 32), :]
        odd = cells[pl.ds(pl.multiple_of(at + 32, 32), 32), :]
        lanes = pl.ds(pl.multiple_of(nn * 128, 128), 128)
        cyc_lhs[pl.ds(pl.multiple_of(m * 32, 32), 32), lanes] = jnp.where(
            low32, even, pltpu.roll(odd, 64, 1)
        ).astype(BF16)
        cyc_lhs[pl.ds(pl.multiple_of(128 + m * 32, 32), 32), lanes] = jnp.where(
            low32, pltpu.roll(even, 64, 1), odd
        ).astype(BF16)
        return carry

    lax.fori_loop(0, 32, pair, 0)
    local[2].wait()

    def product(c):
        lanes = pl.ds(pl.multiple_of(c * 128, 128), 128)
        made = dot(cyc_lhs[...], b_ref[:, lanes])
        for u in range(NSUB):
            part[c, u] = made[u * SUB:(u + 1) * SUB, :]

    up, dn = lax.rem(col + 1, NC), lax.rem(col + NC - 1, NC)
    arms = ((up, slot_up, r_recv_up), (dn, slot_dn, r_recv_dn))

    def target(t, arm):
        return lax.rem(col + (STEPS - t if arm == 0 else NC - STEPS + t), NC)

    def pieces(t, arm):
        if t:
            return range(NSUB)
        return (0, 1) if arm == 0 else (2, 3)

    def ring_copy(t, arm, u):
        device, slots, recv = arms[arm]
        return pltpu.make_async_remote_copy(
            part.at[target(t, arm), u], slots.at[t, u], r_send.at[t, arm, u], recv.at[t, u],
            device_id={"col": device}, device_id_type=MESH,
        )

    product(target(0, 0))
    for arm in (0, 1):
        for u in pieces(0, arm):
            ring_copy(0, arm, u).start()
    for t in range(1, STEPS):
        for arm in (0, 1):
            product(target(t, arm))
        for i in range(NSUB):
            for arm in (0, 1):
                u = i if arm == 0 else (i + 2) % 4
                if u in pieces(t - 1, arm):
                    ring_copy(t - 1, arm, u).wait_recv()
                    c = target(t, arm)
                    part[c, u] = part[c, u] + arms[arm][1][t - 1, u]
                ring_copy(t, arm, u).start()
    product(col)

    def lad_wait(k, carry):
        lad_copy(k).wait_recv()
        return carry

    lax.fori_loop(1, NC, lad_wait, 0)
    total = lad_part[col]
    for k in range(1, NC):
        total = total + lad_slots[k]
    lad_out[...] = total

    for u in range(NSUB):
        for arm in (0, 1):
            ring_copy(STEPS - 1, arm, u).wait_recv()
        par, half = u // 2, u % 2
        cyc_out[pl.ds(par + half * 128, SUB, stride=2), :] = (
            part[col, u] + slot_up[STEPS - 1, u] + slot_dn[STEPS - 1, u]
        )

    def first_sent(k, carry):
        first_stage(k)[1].wait_send()
        return carry

    def tile_sent(k, carry):
        tile_copy(lax.rem(me + k, NR)).wait_send()
        return carry

    def lad_sent(k, carry):
        lad_copy(k).wait_send()
        return carry

    lax.fori_loop(1, 16, first_sent, 0)
    for k in range(1, NX):
        second_copy(k, my_x).wait_send()
    lax.fori_loop(1, NR, tile_sent, 0)
    lax.fori_loop(1, NC, lad_sent, 0)
    for t in range(STEPS):
        for arm in (0, 1):
            for u in pieces(t, arm):
                ring_copy(t, arm, u).wait_send()


def local(
    slab_amps, lad_ints, lad_pairs, cycle_amps, cycle_dest, cycle_block, cycle_kblk, cycle_ints
):
    vmem = pl.BlockSpec(memory_space=pltpu.VMEM)
    hbm = pl.BlockSpec(memory_space=pl.ANY)
    dma = pltpu.SemaphoreType.DMA
    return pl.pallas_call(
        kernel,
        out_shape=(
            jax.ShapeDtypeStruct((64, 128), F32),
            jax.ShapeDtypeStruct((256, 128), F32),
        ),
        in_specs=[vmem] * 5 + [hbm] * 3,
        out_specs=(vmem, vmem),
        scratch_shapes=[
            pltpu.VMEM((ENTRIES, 4096), BF16),
            pltpu.VMEM((TILES, 4096), BF16),
            pltpu.VMEM((1024, 1536), BF16),
            pltpu.VMEM((4096, 128), F32),
            pltpu.VMEM((NR, 64, 128), BF16),
            pltpu.VMEM((NR, 64, 128), BF16),
            pltpu.VMEM((NX, 16, MSG, 128), BF16),
            pltpu.VMEM((NR * MSG, 128), F32),
            pltpu.VMEM((128, 2048), BF16),
            pltpu.VMEM((Q_DEV * 64, ENTRIES), BF16),
            pltpu.VMEM((NC, 2048, 256), BF16),
            pltpu.VMEM((NC, 64, 128), F32),
            pltpu.VMEM((NC, 64, 128), F32),
            pltpu.VMEM((2048, 128), F32),
            pltpu.VMEM((256, 1024), BF16),
            pltpu.VMEM((NC, NSUB, SUB, 128), F32),
            pltpu.VMEM((STEPS, NSUB, SUB, 128), F32),
            pltpu.VMEM((STEPS, NSUB, SUB, 128), F32),
            pltpu.VMEM((64, 64), F32),
            dma((3,)),
            dma((16,)), dma((16,)),
            dma((NX,)), dma((NX,)),
            dma((NR,)), dma((NR,)),
            dma((NC,)), dma((NC,)),
            dma((STEPS, 2, NSUB)), dma((STEPS, NSUB)), dma((STEPS, NSUB)),
        ],
        name="ladder_and_cycle",
        compiler_params=pltpu.CompilerParams(
            collective_id=0, has_side_effects=True, vmem_limit_bytes=52 << 20
        ),
    )(
        slab_amps.reshape(32, 128), lad_pairs.reshape(1, ENTRIES), cycle_dest,
        cycle_block.reshape(1, TILES), cycle_kblk.reshape(1, TILES),
        lad_ints, cycle_amps, cycle_ints,
    )


def solution(mesh):
    in_specs = (
        P("row", "col"),
        P(("row", "col"), None),
        P(("row", "col")),
        P(("row", "col"), None),
        P(("row", "col"), None),
        P(("row", "col")),
        P(("row", "col")),
        P("col", None),
    )
    out_specs = (P(None, ("row", "col")), P("row", "col"))
    return jax.shard_map(local, mesh=mesh, in_specs=in_specs, out_specs=out_specs, check_vma=False)
```

time: 295 us -> 93.3 us (0.32)
  the two profiles are of different devices: /device:TPU:10 before, /device:TPU:64 now
where the time goes in v1:
time: 93.3 us; the launch traced here: 93 us
  Pallas kernels  86.6 us (93%)
  local copies, waits for them, and re-layouts  5.05 us (5%)
    pallas_call x1, Pallas kernels, local(): pl.pallas_call(kernel, out_shape=(jax.ShapeDtypeStruct((64, 128), F32), j...  86.6 us
    unnamed x9, local copies, waits for them, and re-layouts  4.37 us

profile of v1, /device:TPU:64, one launch (start us, length us, event | category | flops | bytes accessed | tf_op | source)
XLA Modules:
  0.0 93.0 jit_solution(18081541227254332331)
XLA Ops:
  0.6 0.7 reshape.17.pairs_ref
  1.3 0.8 reduce
  2.1 0.7 copy.10.dest_ref
  2.8 0.0 copy-start
  2.8 1.0 %copy-done = bf16[64,4096]{1,0:T(8,128)(2,1)S(1)} copy-done((bf16[64,4096]{1,0:T(8,128)(2,1)S(1)}, bf16[64,4096]{1,0:T(8,128)(2,1)}, u32[]{:S(2)}) %copy-start) | copy-done | bytes 524312
  3.9 0.0 copy-start.1
  3.9 0.7 copy-done.1
  4.5 0.0 copy-start.2
  4.5 0.7 copy-done.2
  5.2 86.6 %ladder_and_cycle.1 = (f32[64,128]{1,0:T(8,128)S(1)}, f32[256,128]{1,0:T(8,128)S(1)}) custom-call(bf16[32,128]{1,0:T(8,128)(2,1)S(1)} %bitcast.3, s32[1,384]{1,0:T(1,128)S(1)} %reshape.17.pairs_ref, s32[64,1]{1,0:T(8,128)S(1)} %copy.10.dest_ref, s32[1,64]{1,0:T(1,128)S(1)} %bitcast.4, s32[1,64]{1,0:T(1,128)S(1)} %bitcast.5, bf16[384,4096]{1,0:T(8,128)(2,1)} %w_hbm.1, ...), custom_call_target="tpu_custom_call" | custom-call | tf_op jit(solution)/shard_map/ladder_and_cycle/pallas_call | solution.py:371
  91.8 0.6 copy.13
  92.4 0.7 copy.14
Async XLA Ops:
  2.8 1.0 %copy-start = (bf16[64,4096]{1,0:T(8,128)(2,1)S(1)}, bf16[64,4096]{1,0:T(8,128)(2,1)}, u32[]{:S(2)}) copy-start(bf16[64,4096]{1,0:T(8,128)(2,1)} %cyc_hbm.1) | copy-start | bytes 1572868
  3.9 0.7 copy-start.1
  4.5 0.7 copy-start.2

commit v2 on v1

v2 whole, which is shorter than its diff:
```python
import jax
import jax.numpy as jnp
from jax import lax
from jax.experimental import pallas as pl
from jax.experimental.pallas import tpu as pltpu
from jax.sharding import PartitionSpec as P

MESH = pl.DeviceIdType.MESH
F32 = jnp.float32
BF16 = jnp.bfloat16
I32 = jnp.int32

NR = 64
NC = 12
NY, NX = 8, 4
TILES = 64
ENTRIES = 384
Q_DEV = 24
MSG = 48
SUB = 64
NSUB = 4
STEPS = 6
LADDER_ORDER = (6, 5, 7, 4, 8, 3, 9, 2, 10, 1, 11)
LOW = 3
FIRST = 33
PLACED = 8


def dot(a, b):
    return jnp.dot(a, b, preferred_element_type=F32)


def iota(shape, dim):
    return lax.broadcasted_iota(I32, shape, dim)


def kernel(
    amps_hbm, pairs_hbm, dest_hbm, block_hbm, kblk_hbm, w_hbm, cyc_hbm, b_hbm,
    lad_out, cyc_out,
    amps_ref, pairs_ref, dest_ref, block_ref, kblk_ref,
    w_ref, cyc_ref, b_ref, stage, outgoing, arrived, gather, gstage, lad_lhs, placer, dense,
    lad_part, lad_low, lad_slots, cells, cyc_lhs, part, slot_up, slot_dn, low_out, low_in, turn, lines,
    local_sem, g1_send, g1_recv, g2_send, g2_recv, g3_send, g3_recv, a_send, a_recv, l_send, l_recv,
    r_send, r_recv_up, r_recv_dn,
):
    me = lax.axis_index("row")
    col = lax.axis_index("col")
    my_y = me // 8
    my_x = lax.rem(me // 2, 4)
    my_core = lax.rem(me, 2)

    barrier = pltpu.get_barrier_semaphore()

    def away(i):
        half = i // 2
        return 32 + half - 2 * half * lax.rem(i, 2)

    def greet_row(i, carry):
        pl.semaphore_signal(
            barrier, inc=1, device_id={"row": lax.rem(me + away(i), NR)}, device_id_type=MESH
        )
        return carry

    def greet_col(k, carry):
        pl.semaphore_signal(
            barrier, inc=1, device_id={"col": lax.rem(col + k, NC)}, device_id_type=MESH
        )
        return carry

    lax.fori_loop(1, NR, greet_row, 0)
    lax.fori_loop(1, NC, greet_col, 0)

    local = [
        pltpu.make_async_copy(cyc_hbm, cyc_ref, local_sem.at[0]),
        pltpu.make_async_copy(w_hbm, w_ref, local_sem.at[1]),
        pltpu.make_async_copy(b_hbm, b_ref, local_sem.at[2]),
        pltpu.make_async_copy(dest_hbm, dest_ref, local_sem.at[3]),
        pltpu.make_async_copy(block_hbm, block_ref, local_sem.at[4]),
        pltpu.make_async_copy(kblk_hbm, kblk_ref, local_sem.at[5]),
        pltpu.make_async_copy(amps_hbm, amps_ref, local_sem.at[6]),
        pltpu.make_async_copy(pairs_hbm, pairs_ref, local_sem.at[7]),
    ]
    for i in (3, 4, 5, 6, 0, 7, 1, 2):
        local[i].start()

    local[6].wait()
    for i in range(32):
        lines[i:i + 1, :] = amps_ref[:, i * 128:(i + 1) * 128].astype(F32)
    flipped = lines[...].T
    turn[:, 0:32] = flipped[0:64, :]
    turn[:, 32:64] = flipped[64:128, :]
    quarter = [[turn[pl.ds(2 * a1 + par, 16, stride=4), :] for a1 in (0, 1)] for par in (0, 1)]
    message = jnp.concatenate([jnp.concatenate(quarter[par], axis=1) for par in (0, 1)], axis=0)

    for i in (3, 4, 5):
        local[i].wait()
    dest_row = dest_ref[...]
    eye = iota((TILES, TILES), 0) == iota((TILES, TILES), 1)
    dest_col = jnp.sum(jnp.where(eye, dest_row, 0), axis=1, keepdims=True)
    same = dest_col == dest_row
    earlier_col = iota((TILES, TILES), 0) < iota((TILES, TILES), 1)
    earlier_row = iota((TILES, TILES), 1) < iota((TILES, TILES), 0)
    pos_row = jnp.sum(jnp.where(same & earlier_col, 1, 0), axis=0, keepdims=True)
    pos_col = jnp.sum(jnp.where(same & earlier_row, 1, 0), axis=1, keepdims=True)
    code_row = (block_ref[...] * 16 + kblk_ref[...]).reshape(1, TILES)
    code_col = jnp.sum(jnp.where(eye, code_row, 0), axis=1, keepdims=True)
    slot_row = dest_row * 2 + pos_row
    slot_col = dest_col * 2 + pos_col
    chosen = (iota((2 * NR, TILES), 0) == slot_row).astype(F32).astype(BF16)
    codes = jnp.sum(
        jnp.where(iota((TILES, 2 * NR), 1) == slot_col, code_col + 1, 0), axis=0, keepdims=True
    ) - 1
    gather[my_core, my_x, my_y, 0:32, :] = message.astype(BF16)
    gather[my_core, my_x, my_y, 32:48, :] = jnp.where(
        iota((16, 128), 0) == 0, codes, 0
    ).astype(F32).astype(BF16)

    local[0].wait()

    def stage_tiles(g, carry):
        picked = dot(chosen, cyc_ref[:, pl.ds(pl.multiple_of(g * 256, 256), 256)])
        stage[pl.ds(2 * g, 128, stride=32), :] = picked[:, 0:128]
        stage[pl.ds(2 * g + 1, 128, stride=32), :] = picked[:, 128:256]
        return carry

    lax.fori_loop(0, 16, stage_tiles, 0, unroll=4)

    def tile_fill(d, carry):
        outgoing[d] = stage[pl.ds(pl.multiple_of(d * 64, 64), 64), :].astype(BF16)
        return carry

    lax.fori_loop(0, NR, tile_fill, 0, unroll=4)
    arrived[me] = stage[pl.ds(pl.multiple_of(me * 64, 64), 64), :].astype(BF16)

    def tile_copy(d):
        return pltpu.make_async_remote_copy(
            outgoing.at[d], arrived.at[me], a_send.at[d], a_recv.at[me],
            device_id={"row": d}, device_id_type=MESH,
        )

    def tile_send(i, carry):
        tile_copy(lax.rem(me + away(i), NR)).start()
        return carry

    def first_copy(k, y):
        there = lax.rem(my_y + k, NY)
        ref = gather.at[my_core, my_x, y]
        return pltpu.make_async_remote_copy(
            ref, ref, g1_send.at[k], g1_recv.at[y],
            device_id={"row": there * 8 + my_x * 2 + my_core}, device_id_type=MESH,
        )

    def second_copy(k, x):
        there = lax.rem(my_x + k, NX)
        ref = gather.at[my_core, x]
        return pltpu.make_async_remote_copy(
            ref, ref, g2_send.at[k], g2_recv.at[x],
            device_id={"row": my_y * 8 + there * 2 + my_core}, device_id_type=MESH,
        )

    def third_copy(core):
        ref = gather.at[core]
        return pltpu.make_async_remote_copy(
            ref, ref, g3_send.at[0], g3_recv.at[0],
            device_id={"row": me + 1 - 2 * my_core}, device_id_type=MESH,
        )

    pl.semaphore_wait(barrier, NR - 1 + NC - 1)
    for k in (4, 3, 5, 2, 6, 1, 7):
        first_copy(k, my_y).start()
    lax.fori_loop(1, FIRST, tile_send, 0)

    local[7].wait()
    pairs = pairs_ref[...].reshape(1, ENTRIES)
    p_at = iota((64, ENTRIES), 0)
    p_code = (2 * lax.rem(p_at, 32) + p_at // 32) * Q_DEV

    def build(q, carry):
        placer[pl.ds(pl.multiple_of(q * 64, 64), 64), :] = (
            (p_code + q == pairs).astype(F32).astype(BF16)
        )
        return carry

    lax.fori_loop(0, Q_DEV, build, 0)
    local[1].wait()

    def place(g, carry):
        w_part = w_ref[:, pl.ds(pl.multiple_of(g * 256, 256), 256)]
        for quarter_at in range(4):
            placed = dot(placer[quarter_at * 384:(quarter_at + 1) * 384, :], w_part).astype(BF16)
            for j in range(6):
                q = quarter_at * 6 + j
                for i in (0, 1):
                    dense[
                        q // 2, pl.ds(pl.multiple_of((2 * g + i) * 64, 64), 64),
                        (q % 2) * 128:(q % 2 + 1) * 128,
                    ] = placed[j * 64:(j + 1) * 64, i * 128:(i + 1) * 128]
        return carry

    lax.fori_loop(0, PLACED, place, 0, unroll=2)

    for k in range(1, NY):
        first_copy(k, lax.rem(my_y + k, NY)).wait_recv()
    for k in (2, 1, 3):
        second_copy(k, my_x).start()
    lax.fori_loop(FIRST, NR, tile_send, 0)
    lax.fori_loop(PLACED, 16, place, 0, unroll=2)
    for k in range(1, NX):
        second_copy(k, lax.rem(my_x + k, NX)).wait_recv()
    third_copy(my_core).start()
    third_copy(1 - my_core).wait_recv()

    def widen(i, carry):
        core, x, y = i // 32, lax.rem(i // 8, NX), lax.rem(i, NY)
        row = y * 8 + x * 2 + core
        gstage[pl.ds(pl.multiple_of(row * MSG, MSG), MSG), :] = gather[core, x, y].astype(F32)
        return carry

    lax.fori_loop(0, NR, widen, 0, unroll=4)
    for par in (0, 1):
        for b in range(16):
            lad_lhs[par * 64:(par + 1) * 64, b * 128:(b + 1) * 128] = (
                gstage[pl.ds(par * 16 + b, NR, stride=MSG), :].astype(BF16)
            )

    low = iota((64, 128), 1) < 64

    def lad_copy(k):
        c = lax.rem(col + k, NC)
        return pltpu.make_async_remote_copy(
            lad_low.at[c], lad_slots.at[k], l_send.at[k], l_recv.at[k],
            device_id={"col": c}, device_id_type=MESH,
        )

    def ladder(k):
        c = lax.rem(col + k, NC)
        acc = dot(lad_lhs[...], dense[c])
        first = acc[0:64, 0:128] + pltpu.roll(acc[64:128, 0:128], 64, 1)
        second = pltpu.roll(acc[0:64, 128:256], 64, 1) + acc[64:128, 128:256]
        total = jnp.where(low, first, second)
        if k == 0:
            lad_part[...] = total
        else:
            lad_low[c] = total.astype(BF16)

    def ladder_send(k):
        ladder(k)
        lad_copy(k).start()

    for k in LADDER_ORDER:
        ladder_send(k)
    ladder(0)

    all_codes = gstage[pl.ds(32, NR, stride=MSG), :]
    mine = []
    for j in (0, 1):
        here = jnp.where(iota((NR, 128), 1) == 2 * me + j, all_codes, 0.0)
        mine.append(jnp.sum(here, axis=1, keepdims=True))
    slot_codes = jnp.concatenate(mine, axis=0)
    put = (slot_codes == iota((2 * NR, 128), 1).astype(F32)).astype(F32).T[0:64, :].astype(BF16)

    def tile_wait(i, carry):
        k = away(i)
        s = lax.rem(me + NR - k, NR)
        pltpu.make_async_remote_copy(
            outgoing.at[s], arrived.at[s], a_send.at[s], a_recv.at[s],
            device_id={"row": lax.rem(me + k, NR)}, device_id_type=MESH,
        ).wait_recv()
        stage[pl.ds(pl.multiple_of(s * 64, 64), 64), :] = arrived[s].astype(F32)
        return carry

    stage[pl.ds(pl.multiple_of(me * 64, 64), 64), :] = arrived[me].astype(F32)
    lax.fori_loop(1, NR, tile_wait, 0)

    def cell(g, carry):
        wide = []
        for i in (0, 1):
            a = 2 * g + i
            wide.append(jnp.concatenate(
                [stage[pl.ds(a + 32 * j, NR, stride=64), :] for j in (0, 1)], axis=0
            ).astype(BF16))
        summed = dot(put, jnp.concatenate(wide, axis=1))
        cells[pl.ds(2 * g, 64, stride=32), :] = summed[:, 0:128]
        cells[pl.ds(2 * g + 1, 64, stride=32), :] = summed[:, 128:256]
        return carry

    lax.fori_loop(0, 16, cell, 0, unroll=8)

    low32 = iota((32, 128), 1) < 64

    def pair(i, carry):
        m, nn = i // 8, lax.rem(i, 8)
        at = pl.multiple_of((m * 16 + 2 * nn) * 32, 32)
        even = cells[pl.ds(at, 32), :]
        odd = cells[pl.ds(pl.multiple_of(at + 32, 32), 32), :]
        lanes = pl.ds(pl.multiple_of(nn * 128, 128), 128)
        cyc_lhs[pl.ds(pl.multiple_of(m * 32, 32), 32), lanes] = jnp.where(
            low32, even, pltpu.roll(odd, 64, 1)
        ).astype(BF16)
        cyc_lhs[pl.ds(pl.multiple_of(128 + m * 32, 32), 32), lanes] = jnp.where(
            low32, pltpu.roll(even, 64, 1), odd
        ).astype(BF16)
        return carry

    lax.fori_loop(0, 32, pair, 0, unroll=8)
    local[2].wait()

    def product(c):
        lanes = pl.ds(pl.multiple_of(c * 128, 128), 128)
        made = dot(cyc_lhs[...], b_ref[:, lanes])
        for u in range(NSUB):
            part[c, u] = made[u * SUB:(u + 1) * SUB, :]

    up, dn = lax.rem(col + 1, NC), lax.rem(col + NC - 1, NC)
    arms = ((up, slot_up, r_recv_up), (dn, slot_dn, r_recv_dn))

    def target(t, arm):
        return lax.rem(col + (STEPS - t if arm == 0 else NC - STEPS + t), NC)

    def pieces(t, arm):
        if t:
            return range(NSUB)
        return (0, 1) if arm == 0 else (2, 3)

    def ring_copy(t, arm, u):
        device, slots, recv = arms[arm]
        if t < LOW:
            source, landing = low_out.at[t, arm, u], low_in.at[t, arm, u]
        else:
            source, landing = part.at[target(t, arm), u], slots.at[t - LOW, u]
        return pltpu.make_async_remote_copy(
            source, landing, r_send.at[t, arm, u], recv.at[t, u],
            device_id={"col": device}, device_id_type=MESH,
        )

    def ring_send(t, arm, u):
        if t < LOW:
            low_out[t, arm, u] = part[target(t, arm), u].astype(BF16)
        ring_copy(t, arm, u).start()

    def landed(t, arm, u):
        ring_copy(t, arm, u).wait_recv()
        return low_in[t, arm, u].astype(F32) if t < LOW else arms[arm][1][t - LOW, u]

    product(target(0, 0))
    for arm in (0, 1):
        for u in pieces(0, arm):
            ring_send(0, arm, u)
    for t in range(1, STEPS):
        for arm in (0, 1):
            product(target(t, arm))
        for i in range(NSUB):
            for arm in (0, 1):
                u = i if arm == 0 else (i + 2) % 4
                if u in pieces(t - 1, arm):
                    c = target(t, arm)
                    part[c, u] = part[c, u] + landed(t - 1, arm, u)
                ring_send(t, arm, u)
    product(col)

    def lad_wait(k, carry):
        lad_copy(k).wait_recv()
        return carry

    lax.fori_loop(1, NC, lad_wait, 0)
    total = lad_part[...]
    for k in range(1, NC):
        total = total + lad_slots[k].astype(F32)
    lad_out[...] = total

    for u in range(NSUB):
        par, half = u // 2, u % 2
        cyc_out[pl.ds(par + half * 128, SUB, stride=2), :] = (
            part[col, u] + landed(STEPS - 1, 0, u) + landed(STEPS - 1, 1, u)
        )

    def tile_sent(k, carry):
        tile_copy(lax.rem(me + k, NR)).wait_send()
        return carry

    def lad_sent(k, carry):
        lad_copy(k).wait_send()
        return carry

    for k in range(1, NY):
        first_copy(k, my_y).wait_send()
    for k in range(1, NX):
        second_copy(k, my_x).wait_send()
    third_copy(my_core).wait_send()
    lax.fori_loop(1, NR, tile_sent, 0)
    lax.fori_loop(1, NC, lad_sent, 0)
    for t in range(STEPS):
        for arm in (0, 1):
            for u in pieces(t, arm):
                ring_copy(t, arm, u).wait_send()


def local(
    slab_amps, lad_ints, lad_pairs, cycle_amps, cycle_dest, cycle_block, cycle_kblk, cycle_ints
):
    vmem = pl.BlockSpec(memory_space=pltpu.VMEM)
    hbm = pl.BlockSpec(memory_space=pl.ANY)
    dma = pltpu.SemaphoreType.DMA
    return pl.pallas_call(
        kernel,
        out_shape=(
            jax.ShapeDtypeStruct((64, 128), F32),
            jax.ShapeDtypeStruct((256, 128), F32),
        ),
        in_specs=[hbm] * 8,
        out_specs=(vmem, vmem),
        scratch_shapes=[
            pltpu.VMEM((1, 4096), BF16),
            pltpu.VMEM((ENTRIES,), I32),
            pltpu.VMEM((1, TILES), I32),
            pltpu.VMEM((TILES,), I32),
            pltpu.VMEM((TILES,), I32),
            pltpu.VMEM((ENTRIES, 4096), BF16),
            pltpu.VMEM((TILES, 4096), BF16),
            pltpu.VMEM((1024, 1536), BF16),
            pltpu.VMEM((4096, 128), F32),
            pltpu.VMEM((NR, 64, 128), BF16),
            pltpu.VMEM((NR, 64, 128), BF16),
            pltpu.VMEM((2, NX, NY, MSG, 128), BF16),
            pltpu.VMEM((NR * MSG, 128), F32),
            pltpu.VMEM((128, 2048), BF16),
            pltpu.VMEM((Q_DEV * 64, ENTRIES), BF16),
            pltpu.VMEM((NC, 2048, 256), BF16),
            pltpu.VMEM((64, 128), F32),
            pltpu.VMEM((NC, 64, 128), BF16),
            pltpu.VMEM((NC, 64, 128), BF16),
            pltpu.VMEM((2048, 128), F32),
            pltpu.VMEM((256, 1024), BF16),
            pltpu.VMEM((NC, NSUB, SUB, 128), F32),
            pltpu.VMEM((STEPS - LOW, NSUB, SUB, 128), F32),
            pltpu.VMEM((STEPS - LOW, NSUB, SUB, 128), F32),
            pltpu.VMEM((max(LOW, 1), 2, NSUB, SUB, 128), BF16),
            pltpu.VMEM((max(LOW, 1), 2, NSUB, SUB, 128), BF16),
            pltpu.VMEM((64, 64), F32),
            pltpu.VMEM((32, 128), F32),
            dma((8,)),
            dma((NY,)), dma((NY,)),
            dma((NX,)), dma((NX,)),
            dma((1,)), dma((1,)),
            dma((NR,)), dma((NR,)),
            dma((NC,)), dma((NC,)),
            dma((STEPS, 2, NSUB)), dma((STEPS, NSUB)), dma((STEPS, NSUB)),
        ],
        name="ladder_and_cycle",
        compiler_params=pltpu.CompilerParams(
            collective_id=0, has_side_effects=True, vmem_limit_bytes=60 << 20
        ),
    )(
        slab_amps, lad_pairs, cycle_dest.reshape(1, TILES), cycle_block, cycle_kblk,
        lad_ints, cycle_amps, cycle_ints,
    )


def solution(mesh):
    in_specs = (
        P("row", "col"),
        P(("row", "col"), None),
        P(("row", "col")),
        P(("row", "col"), None),
        P(("row", "col"), None),
        P(("row", "col")),
        P(("row", "col")),
        P("col", None),
    )
    out_specs = (P(None, ("row", "col")), P("row", "col"))
    return jax.shard_map(local, mesh=mesh, in_specs=in_specs, out_specs=out_specs, check_vma=False)
```

time: 93.3 us -> 79.3 us (0.85)
  the two profiles are of different devices: /device:TPU:64 before, /device:TPU:8 now
where the time goes in v2:
time: 79.3 us; the launch traced here: 79.1 us
  Pallas kernels  75.5 us (95%)
  local copies, waits for them, and re-layouts  2.94 us (4%)
    pallas_call x1, Pallas kernels, local(): pl.pallas_call(kernel, out_shape=(jax.ShapeDtypeStruct((64, 128), F32), j...  75.5 us
    unnamed x2, local copies, waits for them, and re-layouts  2.94 us

profile of v2, /device:TPU:8, one launch (start us, length us, event | category | flops | bytes accessed | tf_op | source)
XLA Modules:
  0.0 79.1 jit_solution(999412319741990435)
XLA Ops:
  0.6 75.5 %ladder_and_cycle.1 = (f32[64,128]{1,0:T(8,128)}, f32[256,128]{1,0:T(8,128)}) custom-call(bf16[1,4096]{1,0:T(2,128)(2,1)} %amps_hbm.1, s32[384]{0:T(512)} %pairs_hbm.1, s32[1,64]{1,0:T(1,128)} %bitcast.1, s32[64]{0:T(128)} %block_hbm.1, s32[64]{0:T(128)} %kblk_hbm.1, bf16[384,4096]{1,0:T(8,128)(2,1)} %w_hbm.1, bf16[64,4096]{1,0:T(8,128)(2,1)} %cyc_hbm.1, ...), custom_call_target="tpu_custom_call" | custom-call | tf_op jit(solution)/shard_map/ladder_and_cycle/pallas_call | solution.py:404
  76.2 1.4 %copy.12 = f32[64,128]{1,0:T(8,128)} copy(f32[64,128]{1,0:T(8,128)} %get-tuple-element.4) | data formatting | bytes 65536
  77.6 1.6 %copy.13 = f32[256,128]{1,0:T(8,128)} copy(f32[256,128]{1,0:T(8,128)} %get-tuple-element.5) | data formatting | bytes 262144

commit v3 on v2

--- a/solution.py
+++ b/solution.py
@@ -20,6 +20,7 @@
 SUB = 64
 NSUB = 4
 STEPS = 6
+JOIN = 4
 LADDER_ORDER = (6, 5, 7, 4, 8, 3, 9, 2, 10, 1, 11)
 LOW = 3
 FIRST = 33
@@ -311,8 +312,7 @@
         for u in range(NSUB):
             part[c, u] = made[u * SUB:(u + 1) * SUB, :]
 
-    up, dn = lax.rem(col + 1, NC), lax.rem(col + NC - 1, NC)
-    arms = ((up, slot_up, r_recv_up), (dn, slot_dn, r_recv_dn))
+    arms = ((slot_up, r_recv_up), (slot_dn, r_recv_dn))
 
     def target(t, arm):
         return lax.rem(col + (STEPS - t if arm == 0 else NC - STEPS + t), NC)
@@ -323,7 +323,9 @@
         return (0, 1) if arm == 0 else (2, 3)
 
     def ring_copy(t, arm, u):
-        device, slots, recv = arms[arm]
+        hop = max(STEPS - t - JOIN, 1)
+        device = lax.rem(col + (hop if arm == 0 else NC - hop), NC)
+        slots, recv = arms[arm]
         if t < LOW:
             source, landing = low_out.at[t, arm, u], low_in.at[t, arm, u]
         else:
@@ -340,7 +342,7 @@
 
     def landed(t, arm, u):
         ring_copy(t, arm, u).wait_recv()
-        return low_in[t, arm, u].astype(F32) if t < LOW else arms[arm][1][t - LOW, u]
+        return low_in[t, arm, u].astype(F32) if t < LOW else arms[arm][0][t - LOW, u]
 
     product(target(0, 0))
     for arm in (0, 1):
@@ -352,9 +354,11 @@
         for i in range(NSUB):
             for arm in (0, 1):
                 u = i if arm == 0 else (i + 2) % 4
-                if u in pieces(t - 1, arm):
-                    c = target(t, arm)
-                    part[c, u] = part[c, u] + landed(t - 1, arm, u)
+                c = target(t, arm)
+                came = range(t) if t == STEPS - JOIN else (t - 1,) if t > STEPS - JOIN else ()
+                for past in came:
+                    if u in pieces(past, arm):
+                        part[c, u] = part[c, u] + landed(past, arm, u)
                 ring_send(t, arm, u)
     product(col)
 

time: 79.3 us -> 77.4 us (0.976)
  the two profiles are of different devices: /device:TPU:8 before, /device:TPU:2 now
where the time goes in v3:
time: 77.4 us; the launch traced here: 77.2 us
  Pallas kernels  73.6 us (95%)
  local copies, waits for them, and re-layouts  2.94 us (4%)
    pallas_call x1, Pallas kernels, local(): pl.pallas_call(kernel, out_shape=(jax.ShapeDtypeStruct((64, 128), F32), j...  73.6 us
    unnamed x2, local copies, waits for them, and re-layouts  2.94 us

profile of v3, /device:TPU:2, one launch (start us, length us, event | category | flops | bytes accessed | tf_op | source)
XLA Modules:
  0.0 77.2 jit_solution(16017827302207788402)
XLA Ops:
  0.6 73.6 %ladder_and_cycle.1 = (f32[64,128]{1,0:T(8,128)}, f32[256,128]{1,0:T(8,128)}) custom-call(bf16[1,4096]{1,0:T(2,128)(2,1)} %amps_hbm.1, s32[384]{0:T(512)} %pairs_hbm.1, s32[1,64]{1,0:T(1,128)} %bitcast.1, s32[64]{0:T(128)} %block_hbm.1, s32[64]{0:T(128)} %kblk_hbm.1, bf16[384,4096]{1,0:T(8,128)(2,1)} %w_hbm.1, bf16[64,4096]{1,0:T(8,128)(2,1)} %cyc_hbm.1, ...), custom_call_target="tpu_custom_call" | custom-call | tf_op jit(solution)/shard_map/ladder_and_cycle/pallas_call | solution.py:408
  74.3 1.4 %copy.12 = f32[64,128]{1,0:T(8,128)} copy(f32[64,128]{1,0:T(8,128)} %get-tuple-element.4) | data formatting | bytes 65536
  75.6 1.6 %copy.13 = f32[256,128]{1,0:T(8,128)} copy(f32[256,128]{1,0:T(8,128)} %get-tuple-element.5) | data formatting | bytes 262144

commit v4 on v3

--- a/solution.py
+++ b/solution.py
@@ -68,7 +68,7 @@
         )
         return carry
 
-    lax.fori_loop(1, NR, greet_row, 0)
+    lax.fori_loop(1, NR, greet_row, 0, unroll=7)
     lax.fori_loop(1, NC, greet_col, 0)
 
     local = [
@@ -182,7 +182,7 @@
         )
         return carry
 
-    lax.fori_loop(0, Q_DEV, build, 0)
+    lax.fori_loop(0, Q_DEV, build, 0, unroll=4)
     local[1].wait()
 
     def place(g, carry):
@@ -271,7 +271,7 @@
         return carry
 
     stage[pl.ds(pl.multiple_of(me * 64, 64), 64), :] = arrived[me].astype(F32)
-    lax.fori_loop(1, NR, tile_wait, 0)
+    lax.fori_loop(1, NR, tile_wait, 0, unroll=3)
 
     def cell(g, carry):
         wide = []
@@ -372,12 +372,6 @@
         total = total + lad_slots[k].astype(F32)
     lad_out[...] = total
 
-    for u in range(NSUB):
-        par, half = u // 2, u % 2
-        cyc_out[pl.ds(par + half * 128, SUB, stride=2), :] = (
-            part[col, u] + landed(STEPS - 1, 0, u) + landed(STEPS - 1, 1, u)
-        )
-
     def tile_sent(k, carry):
         tile_copy(lax.rem(me + k, NR)).wait_send()
         return carry
@@ -393,6 +387,12 @@
     third_copy(my_core).wait_send()
     lax.fori_loop(1, NR, tile_sent, 0)
     lax.fori_loop(1, NC, lad_sent, 0)
+    for u in range(NSUB):
+        par, half = u // 2, u % 2
+        cyc_out[pl.ds(par + half * 128, SUB, stride=2), :] = (
+            part[col, u] + landed(STEPS - 1, 0, u) + landed(STEPS - 1, 1, u)
+        )
+
     for t in range(STEPS):
         for arm in (0, 1):
             for u in pieces(t, arm):

time: 77.4 us -> 76.4 us (0.987)
  Pallas kernels: 73.6 us -> 72.6 us
    pallas_call x1, Pallas kernels: 73.6 us -> 72.6 us  [local(): pl.pallas_call(kernel, out_shape=(jax.ShapeDtypeStruct((64, 128), F32), j...]
where the time goes in v4:
time: 76.4 us; the launch traced here: 76.2 us
  Pallas kernels  72.6 us (95%)
  local copies, waits for them, and re-layouts  2.94 us (4%)
    pallas_call x1, Pallas kernels, local(): pl.pallas_call(kernel, out_shape=(jax.ShapeDtypeStruct((64, 128), F32), j...  72.6 us
    unnamed x2, local copies, waits for them, and re-layouts  2.94 us

profile of v4, /device:TPU:2, one launch (start us, length us, event | category | flops | bytes accessed | tf_op | source)
XLA Modules:
  0.0 76.2 jit_solution(2887296621020935378)
XLA Ops:
  0.6 72.6 %ladder_and_cycle.1 = (f32[64,128]{1,0:T(8,128)}, f32[256,128]{1,0:T(8,128)}) custom-call(bf16[1,4096]{1,0:T(2,128)(2,1)} %amps_hbm.1, s32[384]{0:T(512)} %pairs_hbm.1, s32[1,64]{1,0:T(1,128)} %bitcast.1, s32[64]{0:T(128)} %block_hbm.1, s32[64]{0:T(128)} %kblk_hbm.1, bf16[384,4096]{1,0:T(8,128)(2,1)} %w_hbm.1, bf16[64,4096]{1,0:T(8,128)(2,1)} %cyc_hbm.1, ...), custom_call_target="tpu_custom_call" | custom-call | tf_op jit(solution)/shard_map/ladder_and_cycle/pallas_call | solution.py:408
  73.2 1.4 %copy.12 = f32[64,128]{1,0:T(8,128)} copy(f32[64,128]{1,0:T(8,128)} %get-tuple-element.4) | data formatting | bytes 65536
  74.6 1.6 %copy.13 = f32[256,128]{1,0:T(8,128)} copy(f32[256,128]{1,0:T(8,128)} %get-tuple-element.5) | data formatting | bytes 262144

commit v5 on v4

--- a/solution.py
+++ b/solution.py
@@ -250,7 +250,6 @@
 
     for k in LADDER_ORDER:
         ladder_send(k)
-    ladder(0)
 
     all_codes = gstage[pl.ds(32, NR, stride=MSG), :]
     mine = []
@@ -285,7 +284,7 @@
         cells[pl.ds(2 * g + 1, 64, stride=32), :] = summed[:, 128:256]
         return carry
 
-    lax.fori_loop(0, 16, cell, 0, unroll=8)
+    lax.fori_loop(0, 16, cell, 0, unroll=16)
 
     low32 = iota((32, 128), 1) < 64
 
@@ -367,6 +366,7 @@
         return carry
 
     lax.fori_loop(1, NC, lad_wait, 0)
+    ladder(0)
     total = lad_part[...]
     for k in range(1, NC):
         total = total + lad_slots[k].astype(F32)

time: 76.4 us -> 76.6 us (level)
  no operation moved by 1% of the time
where the time goes in v5:
time: 76.6 us; the launch traced here: 76.4 us
  Pallas kernels  72.8 us (95%)
  local copies, waits for them, and re-layouts  2.94 us (4%)
    pallas_call x1, Pallas kernels, local(): pl.pallas_call(kernel, out_shape=(jax.ShapeDtypeStruct((64, 128), F32), j...  72.8 us
    unnamed x2, local copies, waits for them, and re-layouts  2.94 us

profile of v5, /device:TPU:2, one launch (start us, length us, event | category | flops | bytes accessed | tf_op | source)
XLA Modules:
  0.0 76.4 jit_solution(10304789257133131241)
XLA Ops:
  0.6 72.8 %ladder_and_cycle.1 = (f32[64,128]{1,0:T(8,128)}, f32[256,128]{1,0:T(8,128)}) custom-call(bf16[1,4096]{1,0:T(2,128)(2,1)} %amps_hbm.1, s32[384]{0:T(512)} %pairs_hbm.1, s32[1,64]{1,0:T(1,128)} %bitcast.1, s32[64]{0:T(128)} %block_hbm.1, s32[64]{0:T(128)} %kblk_hbm.1, bf16[384,4096]{1,0:T(8,128)(2,1)} %w_hbm.1, bf16[64,4096]{1,0:T(8,128)(2,1)} %cyc_hbm.1, ...), custom_call_target="tpu_custom_call" | custom-call | tf_op jit(solution)/shard_map/ladder_and_cycle/pallas_call | solution.py:408
  73.4 1.4 %copy.12 = f32[64,128]{1,0:T(8,128)} copy(f32[64,128]{1,0:T(8,128)} %get-tuple-element.4) | data formatting | bytes 65536
  74.8 1.6 %copy.13 = f32[256,128]{1,0:T(8,128)} copy(f32[256,128]{1,0:T(8,128)} %get-tuple-element.5) | data formatting | bytes 262144
